TPU v7x, 32 devices: a whole 2x2x4 slice. The times are simulated.
32 devices in a mesh: doc: 16 (over z, y, core), head: 2 (over x).
Axes of the slice: x: 2, y: 2, z: 4, core: 2. Of those that a mesh axis runs over, the one named last changes fastest.
Arguments:
- queries: bfloat16 [8192, 4096], P('doc', 'head'), may hold values from -6 to 6
- local_keys: bfloat16 [8192, 4096], P('doc', 'head'), may hold values from -6 to 6
- local_values: bfloat16 [8192, 4096], P('doc', 'head'), may hold values from -6 to 6
- mem_keys: bfloat16 [16384, 4096], P('doc', 'head'), may hold values from -6 to 6
- mem_values: bfloat16 [16384, 4096], P('doc', 'head'), may hold values from -6 to 6
- offsets: int32 [16, 4], P('doc'), may hold values from 1 to 4
- mem_lengths: int32 [16], replicated, may hold values from 1 to 1024
- out_weight: bfloat16 [4096, 2048], P('head'), may hold values from -0.09375 to 0.09375
Outputs:
- mixed: bfloat16 [8192, 2048], P(('doc', 'head'))
All inputs are finite; a program needn't handle non-finite values.
Results may differ from a plain program's by a relative error of at most 0.015.
Values may be sent and summed in bfloat16 or wider, within the bound.
A program may use at most 320 MiB of HBM per device.

v0:
```python
import math

import jax
import jax.numpy as jnp
from jax import lax
from jax.sharding import PartitionSpec as P

DH = 128


def shifted(value, axis, steps):
    count = lax.axis_size(axis)
    pairs = [(source, (source + steps) % count) for source in range(count)]
    return lax.ppermute(value, axis, pairs)


def split_heads(rows, local_heads):
    return rows.reshape(rows.shape[0], local_heads, DH).transpose(1, 0, 2)


def masked_scores(query_heads, key_heads, live_mask):
    scores = jnp.einsum(
        "hqd,hkd->hqk", query_heads, key_heads, preferred_element_type=jnp.float32
    ) * (1.0 / math.sqrt(DH))
    return jnp.where(live_mask[None], scores, -1e30)


def weighted_values(scores, live_mask, top, total, value_heads):
    exponent = jnp.where(live_mask[None], jnp.exp(scores - top[:, :, None]), 0.0)
    weights = (exponent / total[:, :, None]).astype(jnp.bfloat16)
    return jnp.einsum("hqk,hkd->hqd", weights, value_heads, preferred_element_type=jnp.float32)


def per_device(
    queries, local_keys, local_values, mem_keys, mem_values, offsets, mem_lengths, out_weight
):
    document = lax.axis_index("doc")
    local_heads = queries.shape[1] // DH
    query_count = queries.shape[0]
    memory_rows = mem_keys.shape[0]
    slot_count = offsets.shape[1]
    table_index = jnp.arange(mem_lengths.shape[0])
    causal = jnp.arange(query_count)[:, None] >= jnp.arange(query_count)[None, :]
    own_length = jnp.sum(jnp.where(table_index == document, mem_lengths, 0))
    memory_live = jnp.arange(memory_rows) < own_length
    memory_mask = jnp.broadcast_to(memory_live[None, :], (query_count, memory_rows))
    near_mask = jnp.concatenate([causal, memory_mask], axis=1)
    query_heads = split_heads(queries, local_heads)
    near_keys = split_heads(jnp.concatenate([local_keys, mem_keys], axis=0), local_heads)
    near_values = split_heads(jnp.concatenate([local_values, mem_values], axis=0), local_heads)
    memory_key_heads = split_heads(mem_keys, local_heads)
    memory_value_heads = split_heads(mem_values, local_heads)
    near_scores = masked_scores(query_heads, near_keys, near_mask)
    near_top = jnp.max(near_scores, axis=-1)
    near_sum = jnp.sum(
        jnp.where(near_mask[None], jnp.exp(near_scores - near_top[:, :, None]), 0.0), axis=-1
    )
    visitor_scores = []
    far_tops = []
    far_sums = []
    for distance in range(1, slot_count + 1):
        visiting = shifted(queries, "doc", -distance)
        scores = masked_scores(split_heads(visiting, local_heads), memory_key_heads, memory_mask)
        block_top = jnp.max(scores, axis=-1)
        block_sum = jnp.sum(
            jnp.where(memory_mask[None], jnp.exp(scores - block_top[:, :, None]), 0.0), axis=-1
        )
        visitor_scores.append(scores)
        back_top, back_sum = shifted((block_top, block_sum), "doc", distance)
        far_tops.append(back_top)
        far_sums.append(back_sum)
    uses = [
        jnp.sum((offsets[0] == distance).astype(jnp.float32))
        for distance in range(1, slot_count + 1)
    ]
    top = near_top
    for slot in range(slot_count):
        top = jnp.maximum(top, jnp.where(uses[slot] > 0.0, far_tops[slot], -1e30))
    total = near_sum * jnp.exp(near_top - top)
    for slot in range(slot_count):
        total = total + jnp.where(
            uses[slot] > 0.0,
            uses[slot] * far_sums[slot] * jnp.exp(jnp.minimum(far_tops[slot] - top, 0.0)),
            0.0,
        )
    summed = weighted_values(near_scores, near_mask, top, total, near_values)
    for distance in range(1, slot_count + 1):
        owner_top, owner_total = shifted((top, total), "doc", -distance)
        partial_value = weighted_values(
            visitor_scores[distance - 1], memory_mask, owner_top, owner_total, memory_value_heads
        )
        returned = shifted(partial_value.astype(jnp.bfloat16), "doc", distance).astype(
            partial_value.dtype
        )
        summed = summed + uses[distance - 1] * returned
    attended = summed.astype(jnp.bfloat16).transpose(1, 0, 2).reshape(query_count, local_heads * DH)
    return lax.psum_scatter(
        jnp.dot(attended, out_weight, preferred_element_type=jnp.float32).astype(jnp.bfloat16),
        "head",
        scatter_dimension=0,
        tiled=True,
    )


def solution(mesh):
    in_specs = (
        P("doc", "head"),
        P("doc", "head"),
        P("doc", "head"),
        P("doc", "head"),
        P("doc", "head"),
        P("doc", None),
        P(),
        P("head", None),
    )
    out_specs = P(("doc", "head"), None)
    return jax.shard_map(
        per_device, mesh=mesh, in_specs=in_specs, out_specs=out_specs, check_vma=False
    )
```

profile of v0, /device:TPU:0, one launch (start us, length us, event | category | flops | bytes accessed | tf_op | source)
XLA Modules:
  0.0 557.1 jit_solution(12662698584192713431)
XLA Ops:
  10.5 5.4 collective-permute-start
  19.3 6.4 %copy.19 = bf16[1024,2048]{0,1:T(8,128)(2,1)} copy(bf16[1024,2048]{1,0:T(8,128)(2,1)} %param.11) | data formatting | bytes 8388608 | tf_op args[3]
  33.8 8.8 %copy.20 = bf16[1536,16,128]{2,0,1:T(8,128)(2,1)} copy(bf16[1536,16,128]{0,2,1:T(8,128)(2,1)} %bitcast.139) | data formatting | bytes 12582912 | tf_op jit(solution)/shard_map/reshape | solution.py:18
  42.9 21.3 %fusion = (f32[16,512]{1,0:T(8,128)S(1)}, f32[16,1536,512]{2,1,0:T(8,128)}) fusion(pred[512,1536]{0,1:T(8,128)(4,1)S(1)} %pad_add_fusion, bf16[1536,16,128]{2,0,1:T(8,128)(2,1)} %copy.20, bf16[512,2048]{1,0:T(8,128)(2,1)S(1)} %copy-done.2), kind=kOutput, calls=%fused_computation.3 | convolution fusion | flops 3258966016 | bytes 59539456 | tf_op jit(solution)/shard_map/hqd,hkd->hqk/dot_general | solution.py:22
  67.2 15.7 %fusion.1 = (f32[16,512]{1,0:T(8,128)S(1)}, f32[16,512,1024]{2,1,0:T(8,128)}) fusion(pred[1024]{0:T(1024)(128)(4,1)S(1)} %iota_compare_fusion.1, bf16[512,16,128]{2,0,1:T(8,128)(2,1)S(1)} %copy.23, bf16[1024,2048]{1,0:T(8,128)(2,1)} %param.11), kind=kOutput, calls=%fused_computation.16 | convolution fusion | flops 2172641280 | bytes 39879680 | tf_op jit(solution)/shard_map/hqd,hkd->hqk/dot_general | solution.py:22
  83.0 24.2 %collective-permute-done.6 = bf16[512,2048]{0,1:T(8,128)(2,1)} collective-permute-done((bf16[512,2048]{0,1:T(8,128)(2,1)}, bf16[512,2048]{0,1:T(8,128)(2,1)}, u32[]{:S(2)}, u32[]{:S(2)}) %collective-permute-start.6) | collective-permute-done | bytes 2097184 | tf_op jit(solution)/shard_map/ppermute | solution.py:14
  110.2 15.3 %fusion.12 = f32[16,512,1024]{2,1,0:T(8,128)} fusion(bf16[512,16,128]{2,0,1:T(8,128)(2,1)S(1)} %copy.30, bf16[1024,2048]{1,0:T(8,128)(2,1)} %param.11), kind=kOutput, calls=%fused_computation.31 | convolution fusion | flops 2147483648 | bytes 39845888 | tf_op jit(solution)/shard_map/hqd,hkd->hqk/dot_general | solution.py:22
  125.5 25.8 %collective-permute-done.4 = bf16[512,2048]{0,1:T(8,128)(2,1)} collective-permute-done((bf16[512,2048]{0,1:T(8,128)(2,1)}, bf16[512,2048]{0,1:T(8,128)(2,1)}, u32[]{:S(2)}, u32[]{:S(2)}) %collective-permute-start.4) | collective-permute-done | bytes 2097184 | tf_op jit(solution)/shard_map/ppermute | solution.py:14
  154.3 15.5 %fusion.13 = f32[16,512,1024]{2,1,0:T(8,128)} fusion(bf16[512,16,128]{2,0,1:T(8,128)(2,1)S(1)} %copy.28, bf16[1024,2048]{1,0:T(8,128)(2,1)} %param.11), kind=kOutput, calls=%fused_computation.32 | convolution fusion | flops 2147483648 | bytes 39845888 | tf_op jit(solution)/shard_map/hqd,hkd->hqk/dot_general | solution.py:22
  176.8 46.3 %select_reduce_fusion.4 = (f32[16,512]{1,0:T(8,128)S(1)}, f32[16,512]{1,0:T(8,128)S(1)}, f32[16,512]{1,0:T(8,128)S(1)}, f32[16,512]{1,0:T(8,128)S(1)}, f32[16,512,1024]{2,1,0:T(8,128)}) fusion(f32[16,512,1024]{2,1,0:T(8,128)} %get-tuple-element.19, f32[16,512]{1,0:T(8,128)S(1)} %get-tuple-element.18, pred[1024]{0:T(1024)(128)(4,1)S(1)} %iota_compare_fusion.1, ...), kind=kOutput, calls=%fused_computation.11 | convolution fusion | flops 2264891392 | bytes 140674048 | tf_op jit(solution)/shard_map/hqd,hkd->hqk/dot_general | solution.py:22
  223.1 36.0 %select_reduce_fusion.3 = (f32[16,512]{1,0:T(8,128)S(1)}, f32[16,512]{1,0:T(8,128)S(1)}, f32[16,512]{1,0:T(8,128)S(1)}) fusion(f32[16,512,1024]{2,1,0:T(8,128)} %get-tuple-element.20, f32[16,512]{1,0:T(8,128)S(1)} %get-tuple-element.6, pred[1024]{0:T(1024)(128)(4,1)S(1)} %iota_compare_fusion.1, f32[16,512]{1,0:T(8,128)S(1)} %get-tuple-element.7, ...), kind=kLoop, calls=%fused_computation.10 | loop fusion | flops 125804544 | bytes 100860928 | tf_op jit(solution)/shard_map/reduce_sum | solution.py:65
  261.1 21.8 %select_reduce_fusion = f32[16,512]{1,0:T(8,128)S(1)} fusion(f32[16,1536,512]{2,1,0:T(8,128)} %get-tuple-element.22, f32[16,512]{1,0:T(8,128)S(1)} %get-tuple-element.21, pred[512,1536]{0,1:T(8,128)(4,1)S(1)} %pad_add_fusion), kind=kLoop, calls=%fused_computation.2 | loop fusion | flops 62906368 | bytes 51183616 | tf_op jit(solution)/shard_map/reduce_sum | solution.py:55
  299.9 5.9 %pad_maximum_fusion = bf16[1536,2048]{1,0:T(8,128)(2,1)} fusion(bf16[1024,2048]{1,0:T(8,128)(2,1)} %param.12, bf16[512,2048]{1,0:T(8,128)(2,1)S(1)} %copy-done.4), kind=kLoop, calls=%fused_computation.25 | loop fusion | flops 12582912 | bytes 12582912 | tf_op jit(solution)/shard_map/concatenate | solution.py:50
  305.8 8.8 %copy.31 = bf16[1536,2048]{0,1:T(8,128)(2,1)} copy(bf16[1536,2048]{1,0:T(8,128)(2,1)} %pad_maximum_fusion) | data formatting | bytes 12582912 | tf_op jit(solution)/shard_map/concatenate | solution.py:50
  320.5 17.5 %fusion.32 = bf16[16,512,128]{1,2,0:T(8,128)(2,1)} fusion(f32[16,512,1024]{2,1,0:T(8,128)} %get-tuple-element.19, f32[16,512]{1,0:T(8,128)S(1)} %collective-permute-done.13, f32[16,512]{1,0:T(8,128)S(1)} %collective-permute-done.12, pred[1024]{0:T(1024)(128)(4,1)S(1)} %iota_compare_fusion.1, bf16[1024,2048]{1,0:T(8,128)(2,1)} %param.12), kind=kOutput, calls=%fused_computation.55 | convolution fusion | flops 2198863872 | bytes 39912448 | tf_op jit(solution)/shard_map/hqk,hkd->hqd/dot_general | solution.py:31
  339.8 16.1 %fusion.31 = bf16[16,512,128]{1,2,0:T(8,128)(2,1)} fusion(f32[16,512,1024]{2,1,0:T(8,128)} %get-tuple-element.20, f32[16,512]{1,0:T(8,128)S(1)} %collective-permute-done.16, f32[16,512]{1,0:T(8,128)S(1)} %collective-permute-done.15, pred[1024]{0:T(1024)(128)(4,1)S(1)} %iota_compare_fusion.1, bf16[1024,2048]{1,0:T(8,128)(2,1)S(1)} %copy-done.3), kind=kOutput, calls=%fused_computation.54 | convolution fusion | flops 2198863872 | bytes 39912448 | tf_op jit(solution)/shard_map/hqk,hkd->hqd/dot_general | solution.py:31
  356.4 16.2 %fusion.30 = bf16[16,512,128]{1,2,0:T(8,128)(2,1)} fusion(f32[16,512,1024]{2,1,0:T(8,128)} %fusion.13, f32[16,512]{1,0:T(8,128)S(1)} %collective-permute-done.19, f32[16,512]{1,0:T(8,128)S(1)} %collective-permute-done.18, pred[1024]{0:T(1024)(128)(4,1)S(1)} %iota_compare_fusion.1, bf16[1024,2048]{1,0:T(8,128)(2,1)S(1)} %copy-done.3), kind=kOutput, calls=%fused_computation.53 | convolution fusion | flops 2198863872 | bytes 39912448 | tf_op jit(solution)/shard_map/hqk,hkd->hqd/dot_general | solution.py:31
  373.6 16.1 %fusion.29 = bf16[16,512,128]{1,2,0:T(8,128)(2,1)} fusion(f32[16,512,1024]{2,1,0:T(8,128)} %fusion.12, f32[16,512]{1,0:T(8,128)S(1)} %collective-permute-done.22, f32[16,512]{1,0:T(8,128)} %collective-permute-done.21, pred[1024]{0:T(1024)(128)(4,1)S(1)} %iota_compare_fusion.1, bf16[1024,2048]{1,0:T(8,128)(2,1)S(1)} %copy-done.3), kind=kOutput, calls=%fused_computation.52 | convolution fusion | flops 2198863872 | bytes 39912448 | tf_op jit(solution)/shard_map/hqk,hkd->hqd/dot_general | solution.py:31
  390.7 23.8 %fusion.5 = f32[16,512,128]{1,2,0:T(8,128)} fusion(bf16[16,1536,128]{1,2,0:T(8,128)(2,1)S(1)} %bitcast.142, f32[16,1536,512]{2,1,0:T(8,128)} %get-tuple-element.22, f32[16,512]{1,0:T(8,128)} %get-tuple-element.17, f32[16,512]{1,0:T(8,128)} %get-tuple-element.16, pred[512,1536]{0,1:T(8,128)(4,1)S(1)} %copy-done.1), kind=kOutput, calls=%fused_computation.20 | convolution fusion | flops 3296722944 | bytes 61669376 | tf_op jit(solution)/shard_map/hqk,hkd->hqd/dot_general | solution.py:31
  414.6 16.4 %collective-permute-done.20 = bf16[16,512,128]{1,2,0:T(8,128)(2,1)} collective-permute-done((bf16[16,512,128]{1,2,0:T(8,128)(2,1)}, bf16[16,512,128]{1,2,0:T(8,128)(2,1)}, u32[]{:S(2)}, u32[]{:S(2)}) %collective-permute-start.20) | collective-permute-done | bytes 2097184 | tf_op jit(solution)/shard_map/ppermute | solution.py:14
  431.0 9.6 %collective-permute-done.23 = bf16[16,512,128]{1,2,0:T(8,128)(2,1)} collective-permute-done((bf16[16,512,128]{1,2,0:T(8,128)(2,1)}, bf16[16,512,128]{1,2,0:T(8,128)(2,1)}, u32[]{:S(2)}, u32[]{:S(2)}) %collective-permute-start.23) | collective-permute-done | bytes 2097184 | tf_op jit(solution)/shard_map/ppermute | solution.py:14
  440.6 8.9 %add_convert_fusion = bf16[16,512,128]{1,2,0:T(8,128)(2,1)S(1)} fusion(bf16[16,512,128]{1,2,0:T(8,128)(2,1)} %collective-permute-done.23, bf16[16,512,128]{1,2,0:T(8,128)(2,1)} %collective-permute-done.20, bf16[16,512,128]{1,2,0:T(8,128)(2,1)} %collective-permute-done.17, f32[16,512,128]{1,2,0:T(8,128)} %fusion.5, ...), kind=kLoop, calls=%fused_computation.35 | loop fusion | flops 13631488 | bytes 14680080 | tf_op jit(solution)/shard_map/convert_element_type | solution.py:96
  449.4 9.2 %convolution_convert_fusion = bf16[512,2048]{1,0:T(8,128)(2,1)} fusion(bf16[512,2048]{0,1:T(8,128)(2,1)S(1)} %bitcast.143, bf16[2048,2048]{1,0:T(8,128)(2,1)} %param.15), kind=kOutput, calls=%fused_computation.37 | convolution fusion | flops 4296015872 | bytes 12582912 | tf_op jit(solution)/shard_map/dot_general | solution.py:98
  458.7 91.2 %reduce-scatter.2.cloned.1.call-done = bf16[256,2048]{1,0:T(8,128)(2,1)} async-done(((bf16[512,2048]{1,0:T(8,128)(2,1)}), bf16[256,2048]{1,0:T(8,128)(2,1)}) %reduce-scatter.2.cloned.1.call-update) | async-done | bytes 1048592 | tf_op jit(solution)/shard_map/reduce_scatter | solution.py:97
  (76 shorter events, 58.4 us)
Async XLA Ops:
  6.5 543.3 %reduce-scatter.2.cloned.1.call-start = ((), (), s32[]{:S(2)}) async-start(), calls=%async_computation.1 | async-start | bytes 3145728 | tf_op jit(solution)/shard_map/reduce_scatter | solution.py:97
  10.5 53.7 %collective-permute-start = (bf16[512,2048]{0,1:T(8,128)(2,1)}, bf16[512,2048]{0,1:T(8,128)(2,1)}, u32[]{:S(2)}, u32[]{:S(2)}) collective-permute-start(bf16[512,2048]{0,1:T(8,128)(2,1)} %copy.22), channel_id=1, source_target_pairs={{0,30},{2,0},{4,2},{6,4},{8,6},{10,8},{12,10},{14,12},{16,14},{18,... | collective-permute-start | bytes 6291464 | tf_op jit(solution)/shard_map/ppermute | solution.py:14
  15.9 91.3 %collective-permute-start.6 = (bf16[512,2048]{0,1:T(8,128)(2,1)}, bf16[512,2048]{0,1:T(8,128)(2,1)}, u32[]{:S(2)}, u32[]{:S(2)}) collective-permute-start(bf16[512,2048]{0,1:T(8,128)(2,1)} %copy.22), channel_id=1, source_target_pairs={{0,24},{2,26},{4,28},{6,30},{8,0},{10,2},{12,4},{14,6},{16,8},{18,... | collective-permute-start | bytes 6291464 | tf_op jit(solution)/shard_map/ppermute | solution.py:14
  16.4 134.9 %collective-permute-start.4 = (bf16[512,2048]{0,1:T(8,128)(2,1)}, bf16[512,2048]{0,1:T(8,128)(2,1)}, u32[]{:S(2)}, u32[]{:S(2)}) collective-permute-start(bf16[512,2048]{0,1:T(8,128)(2,1)} %copy.22), channel_id=1, source_target_pairs={{0,26},{2,28},{4,30},{6,0},{8,2},{10,4},{12,6},{14,8},{16,10},{18,... | collective-permute-start | bytes 6291464 | tf_op jit(solution)/shard_map/ppermute | solution.py:14
  16.4 157.4 %collective-permute-start.2 = (bf16[512,2048]{0,1:T(8,128)(2,1)}, bf16[512,2048]{0,1:T(8,128)(2,1)}, u32[]{:S(2)}, u32[]{:S(2)}) collective-permute-start(bf16[512,2048]{0,1:T(8,128)(2,1)} %copy.22), channel_id=1, source_target_pairs={{0,28},{2,30},{4,0},{6,2},{8,4},{10,6},{12,8},{14,10},{16,12},{18,... | collective-permute-start | bytes 6291464 | tf_op jit(solution)/shard_map/ppermute | solution.py:14
  259.1 29.1 %collective-permute-start.10 = (f32[16,512]{1,0:T(8,128)S(1)}, f32[16,512]{1,0:T(8,128)S(1)}, u32[]{:S(2)}, u32[]{:S(2)}) collective-permute-start(f32[16,512]{1,0:T(8,128)S(1)} %get-tuple-element.10), channel_id=1, source_target_pairs={{0,6},{2,8},{4,10},{6,12},{8,14},{10,16},{12,18},{14,20},{16,22},{... | collective-permute-start | bytes 98312 | tf_op jit(solution)/shard_map/ppermute | solution.py:14
  259.2 29.4 %collective-permute-start.11 = (f32[16,512]{1,0:T(8,128)S(1)}, f32[16,512]{1,0:T(8,128)S(1)}, u32[]{:S(2)}, u32[]{:S(2)}) collective-permute-start(f32[16,512]{1,0:T(8,128)S(1)} %get-tuple-element.11), channel_id=1, source_target_pairs={{0,8},{2,10},{4,12},{6,14},{8,16},{10,18},{12,20},{14,22},{16,24},... | collective-permute-start | bytes 98312 | tf_op jit(solution)/shard_map/ppermute | solution.py:14
  259.2 29.3 %collective-permute-start.9 = (f32[16,512]{1,0:T(8,128)S(1)}, f32[16,512]{1,0:T(8,128)S(1)}, u32[]{:S(2)}, u32[]{:S(2)}) collective-permute-start(f32[16,512]{1,0:T(8,128)S(1)} %get-tuple-element.9), channel_id=1, source_target_pairs={{0,4},{2,6},{4,8},{6,10},{8,12},{10,14},{12,16},{14,18},{16,20},{1... | collective-permute-start | bytes 98312 | tf_op jit(solution)/shard_map/ppermute | solution.py:14
  283.0 9.8 %collective-permute-start.3 = (f32[16,512]{1,0:T(8,128)S(1)}, f32[16,512]{1,0:T(8,128)S(1)}, u32[]{:S(2)}, u32[]{:S(2)}) collective-permute-start(f32[16,512]{1,0:T(8,128)S(1)} %get-tuple-element.6), channel_id=1, source_target_pairs={{0,4},{2,6},{4,8},{6,10},{8,12},{10,14},{12,16},{14,18},{16,20},{1... | collective-permute-start | bytes 98312 | tf_op jit(solution)/shard_map/ppermute | solution.py:14
  283.0 9.7 %collective-permute-start.5 = (f32[16,512]{1,0:T(8,128)S(1)}, f32[16,512]{1,0:T(8,128)S(1)}, u32[]{:S(2)}, u32[]{:S(2)}) collective-permute-start(f32[16,512]{1,0:T(8,128)S(1)} %get-tuple-element.7), channel_id=1, source_target_pairs={{0,6},{2,8},{4,10},{6,12},{8,14},{10,16},{12,18},{14,20},{16,22},{... | collective-permute-start | bytes 98312 | tf_op jit(solution)/shard_map/ppermute | solution.py:14
  288.5 6.4 %collective-permute-start.1 = (f32[16,512]{1,0:T(8,128)S(1)}, f32[16,512]{1,0:T(8,128)S(1)}, u32[]{:S(2)}, u32[]{:S(2)}) collective-permute-start(f32[16,512]{1,0:T(8,128)S(1)} %get-tuple-element.18), channel_id=1, source_target_pairs={{0,2},{2,4},{4,6},{6,8},{8,10},{10,12},{12,14},{14,16},{16,18},{18... | collective-permute-start | bytes 98312 | tf_op jit(solution)/shard_map/ppermute | solution.py:14
  288.5 6.4 %collective-permute-start.8 = (f32[16,512]{1,0:T(8,128)S(1)}, f32[16,512]{1,0:T(8,128)S(1)}, u32[]{:S(2)}, u32[]{:S(2)}) collective-permute-start(f32[16,512]{1,0:T(8,128)S(1)} %get-tuple-element.5), channel_id=1, source_target_pairs={{0,2},{2,4},{4,6},{6,8},{8,10},{10,12},{12,14},{14,16},{16,18},{18... | collective-permute-start | bytes 98312 | tf_op jit(solution)/shard_map/ppermute | solution.py:14
  298.1 19.7 %collective-permute-start.12 = (f32[16,512]{1,0:T(8,128)}, f32[16,512]{1,0:T(8,128)S(1)}, u32[]{:S(2)}, u32[]{:S(2)}) collective-permute-start(f32[16,512]{1,0:T(8,128)} %get-tuple-element.16), channel_id=1, source_target_pairs={{0,30},{2,0},{4,2},{6,4},{8,6},{10,8},{12,10},{14,12},{16,14},{18,... | collective-permute-start | bytes 98312 | tf_op jit(solution)/shard_map/ppermute | solution.py:14
  299.4 18.4 %collective-permute-start.13 = (f32[16,512]{1,0:T(8,128)}, f32[16,512]{1,0:T(8,128)S(1)}, u32[]{:S(2)}, u32[]{:S(2)}) collective-permute-start(f32[16,512]{1,0:T(8,128)} %get-tuple-element.17), channel_id=1, source_target_pairs={{0,30},{2,0},{4,2},{6,4},{8,6},{10,8},{12,10},{14,12},{16,14},{18,... | collective-permute-start | bytes 98312 | tf_op jit(solution)/shard_map/ppermute | solution.py:14
  314.6 23.4 %collective-permute-start.15 = (f32[16,512]{1,0:T(8,128)}, f32[16,512]{1,0:T(8,128)S(1)}, u32[]{:S(2)}, u32[]{:S(2)}) collective-permute-start(f32[16,512]{1,0:T(8,128)} %get-tuple-element.16), channel_id=1, source_target_pairs={{0,28},{2,30},{4,0},{6,2},{8,4},{10,6},{12,8},{14,10},{16,12},{18,... | collective-permute-start | bytes 98312 | tf_op jit(solution)/shard_map/ppermute | solution.py:14
  316.1 23.6 %collective-permute-start.16 = (f32[16,512]{1,0:T(8,128)}, f32[16,512]{1,0:T(8,128)S(1)}, u32[]{:S(2)}, u32[]{:S(2)}) collective-permute-start(f32[16,512]{1,0:T(8,128)} %get-tuple-element.17), channel_id=1, source_target_pairs={{0,28},{2,30},{4,0},{6,2},{8,4},{10,6},{12,8},{14,10},{16,12},{18,... | collective-permute-start | bytes 98312 | tf_op jit(solution)/shard_map/ppermute | solution.py:14
  317.8 38.1 %collective-permute-start.18 = (f32[16,512]{1,0:T(8,128)}, f32[16,512]{1,0:T(8,128)S(1)}, u32[]{:S(2)}, u32[]{:S(2)}) collective-permute-start(f32[16,512]{1,0:T(8,128)} %get-tuple-element.16), channel_id=1, source_target_pairs={{0,26},{2,28},{4,30},{6,0},{8,2},{10,4},{12,6},{14,8},{16,10},{18,... | collective-permute-start | bytes 98312 | tf_op jit(solution)/shard_map/ppermute | solution.py:14
  317.8 38.6 %collective-permute-start.19 = (f32[16,512]{1,0:T(8,128)}, f32[16,512]{1,0:T(8,128)S(1)}, u32[]{:S(2)}, u32[]{:S(2)}) collective-permute-start(f32[16,512]{1,0:T(8,128)} %get-tuple-element.17), channel_id=1, source_target_pairs={{0,26},{2,28},{4,30},{6,0},{8,2},{10,4},{12,6},{14,8},{16,10},{18,... | collective-permute-start | bytes 98312 | tf_op jit(solution)/shard_map/ppermute | solution.py:14
  317.8 55.8 %collective-permute-start.21 = (f32[16,512]{1,0:T(8,128)}, f32[16,512]{1,0:T(8,128)}, u32[]{:S(2)}, u32[]{:S(2)}) collective-permute-start(f32[16,512]{1,0:T(8,128)} %get-tuple-element.16), channel_id=1, source_target_pairs={{0,24},{2,26},{4,28},{6,30},{8,0},{10,2},{12,4},{14,6},{16,8},{18,... | collective-permute-start | bytes 98312 | tf_op jit(solution)/shard_map/ppermute | solution.py:14
  338.0 35.6 %collective-permute-start.22 = (f32[16,512]{1,0:T(8,128)}, f32[16,512]{1,0:T(8,128)S(1)}, u32[]{:S(2)}, u32[]{:S(2)}) collective-permute-start(f32[16,512]{1,0:T(8,128)} %get-tuple-element.17), channel_id=1, source_target_pairs={{0,24},{2,26},{4,28},{6,30},{8,0},{10,2},{12,4},{14,6},{16,8},{18,... | collective-permute-start | bytes 98312 | tf_op jit(solution)/shard_map/ppermute | solution.py:14
  339.8 74.8 %collective-permute-start.14 = (bf16[16,512,128]{1,2,0:T(8,128)(2,1)}, bf16[16,512,128]{1,2,0:T(8,128)(2,1)}, u32[]{:S(2)}, u32[]{:S(2)}) collective-permute-start(bf16[16,512,128]{1,2,0:T(8,128)(2,1)} %fusion.32), channel_id=1, source_target_pairs={{0,2},{2,4},{4,6},{6,8},{8,10},{10,12},{12,14},{14,16},{16,18},{18... | collective-permute-start | bytes 6291464 | tf_op jit(solution)/shard_map/ppermute | solution.py:14
  355.8 58.7 %collective-permute-start.17 = (bf16[16,512,128]{1,2,0:T(8,128)(2,1)}, bf16[16,512,128]{1,2,0:T(8,128)(2,1)}, u32[]{:S(2)}, u32[]{:S(2)}) collective-permute-start(bf16[16,512,128]{1,2,0:T(8,128)(2,1)} %fusion.31), channel_id=1, source_target_pairs={{0,4},{2,6},{4,8},{6,10},{8,12},{10,14},{12,16},{14,18},{16,20},{1... | collective-permute-start | bytes 6291464 | tf_op jit(solution)/shard_map/ppermute | solution.py:14
  372.6 58.4 %collective-permute-start.20 = (bf16[16,512,128]{1,2,0:T(8,128)(2,1)}, bf16[16,512,128]{1,2,0:T(8,128)(2,1)}, u32[]{:S(2)}, u32[]{:S(2)}) collective-permute-start(bf16[16,512,128]{1,2,0:T(8,128)(2,1)} %fusion.30), channel_id=1, source_target_pairs={{0,6},{2,8},{4,10},{6,12},{8,14},{10,16},{12,18},{14,20},{16,22},{... | collective-permute-start | bytes 6291464 | tf_op jit(solution)/shard_map/ppermute | solution.py:14
  389.7 50.9 %collective-permute-start.23 = (bf16[16,512,128]{1,2,0:T(8,128)(2,1)}, bf16[16,512,128]{1,2,0:T(8,128)(2,1)}, u32[]{:S(2)}, u32[]{:S(2)}) collective-permute-start(bf16[16,512,128]{1,2,0:T(8,128)(2,1)} %fusion.29), channel_id=1, source_target_pairs={{0,8},{2,10},{4,12},{6,14},{8,16},{10,18},{12,20},{14,22},{16,24},... | collective-permute-start | bytes 6291464 | tf_op jit(solution)/shard_map/ppermute | solution.py:14
  (9 other events, 396.0 us)
Sparse Core Ops, SparseCore 0:
  458.8 91.0 reduce-scatter.1
where the time goes:
time: 567 us; the launch traced here: 557 us
  matrix products  213 us (38%)
  waiting for transfers between devices  173 us (31%)
  other arithmetic  84 us (15%)
  local copies, waits for them, and re-layouts  43 us (8%)
  starting transfers between devices  27.3 us (5%)
  between operations  16.5 us (3%)
    dot_general x5, matrix products, masked_scores(): jnp.einsum('hqd,hkd->hqk', query_heads, key_heads, preferred_element_type...  114 us
    reduce_scatter x1, waiting for transfers between devices, per_device(): lax.psum_scatter(jnp.dot(attended, out_weight, preferred_element_type=jnp...  91.2 us
    dot_general x5, matrix products, weighted_values(): jnp.einsum('hqk,hkd->hqd', weights, value_heads, preferred_element_type=j...  89.7 us
    ppermute x24, waiting for transfers between devices, shifted(): return lax.ppermute(value, axis, pairs)  82.1 us
    reduce_sum x1, other arithmetic, per_device(): jnp.sum(jnp.where(memory_mask[None], jnp.exp(scores - block_top[:, :, Non...  36 us
    ppermute x24, starting transfers between devices, shifted(): return lax.ppermute(value, axis, pairs)  27.3 us
    reduce_sum x1, other arithmetic, per_device(): jnp.sum(jnp.where(near_mask[None], jnp.exp(near_scores - near_top[:, :, N...  21.8 us
    reshape x5, local copies, waits for them, and re-layouts, split_heads(): return rows.reshape(rows.shape[0], local_heads, DH).transpose(1, 0, 2)  20.9 us
  transfers between devices with their start and end apart: 25, of which 8 were waited for; matrix products, arithmetic and copies ran while one was open for 41% of the time, Pallas kernels for 0%

commit v1 on v0

v1 whole, which is shorter than its diff:
```python
import functools
import math

import jax
import jax.numpy as jnp
from jax import lax
from jax.experimental import pallas as pl
from jax.experimental.pallas import tpu as pltpu
from jax.sharding import PartitionSpec as P

DH = 128
SCALE = math.log2(math.e) / math.sqrt(DH)
NEVER = -1e30
CHUNKS = 4
ROWS = 256
HEADS_PER_STEP = 2
VMEM = 48 * 1024 * 1024


def nt_dot(a, b):
    return lax.dot_general(a, b, (((1,), (1,)), ((), ())), preferred_element_type=jnp.float32)


def attend(query, pieces):
    scores = []
    top = None
    for keys, _, live in pieces:
        score = nt_dot(query, keys)
        if live is not None:
            score = jnp.where(live, score, NEVER)
        scores.append(score)
        piece_top = jnp.max(score, axis=1, keepdims=True)
        top = piece_top if top is None else jnp.maximum(top, piece_top)
    total = None
    for score, (_, values, _) in zip(scores, pieces):
        weights = jnp.exp2((score - top) * SCALE).astype(jnp.bfloat16)
        wide = jnp.concatenate([values, jnp.ones_like(values)], axis=1)
        part = jnp.dot(weights, wide, preferred_element_type=jnp.float32)
        total = part if total is None else total + part
    summed = total[:, DH:]
    return total[:, :DH] / summed, top * SCALE + jnp.log2(summed)


def merge(parts):
    top = functools.reduce(jnp.maximum, [log for _, log in parts])
    shares = [jnp.exp2(log - top) for _, log in parts]
    whole = functools.reduce(jnp.add, shares)
    out = functools.reduce(jnp.add, [share * part for share, (part, _) in zip(shares, parts)])
    return out / whole, top + jnp.log2(whole)


def to_rows(row):
    return jnp.broadcast_to(row, (DH, row.shape[1])).T


def to_row(log):
    return log.T[0:1, :]


def memory_pieces(key_ref, value_ref, columns, size, block, length):
    pieces = []
    if size > block:
        rows = pl.ds(0, size - block)
        pieces.append((key_ref[rows, columns], value_ref[rows, columns], None))
    rows = pl.ds(size - block, block)
    index = lax.broadcasted_iota(jnp.int32, (1, block), 1) + (size - block)
    pieces.append((key_ref[rows, columns], value_ref[rows, columns], index < length))
    return pieces


def by_length(length, memory_rows, run):
    block = memory_rows // 4
    for step in range(1, 5):
        size = step * block
        low = length > size - block if step > 1 else True
        high = length <= size if step < 4 else True
        pl.when(jnp.logical_and(low, high))(functools.partial(run, size, block))


def near_kernel(heads, numbers, q_ref, lk_ref, lv_ref, mk_ref, mv_ref, o_ref, log_ref):
    length = numbers[0]
    count = q_ref.shape[0]

    def run(size, block):
        for head in range(heads):
            columns = pl.ds(head * DH, DH)
            for start in range(0, count, ROWS):
                rows = pl.ds(start, ROWS)
                pieces = memory_pieces(mk_ref, mv_ref, columns, size, block, length)
                if start:
                    past = pl.ds(0, start)
                    pieces.append((lk_ref[past, columns], lv_ref[past, columns], None))
                causal = lax.broadcasted_iota(jnp.int32, (ROWS, ROWS), 0) >= (
                    lax.broadcasted_iota(jnp.int32, (ROWS, ROWS), 1)
                )
                pieces.append((lk_ref[rows, columns], lv_ref[rows, columns], causal))
                out, log = attend(q_ref[rows, columns], pieces)
                o_ref[rows, columns] = out.astype(o_ref.dtype)
                log_ref[head, :, rows] = to_row(log)

    by_length(length, mk_ref.shape[0], run)


def visit_kernel(heads, extra, numbers, q_ref, mk_ref, mv_ref, *refs):
    parts, (o_ref, log_ref) = refs[: 2 * extra], refs[2 * extra :]
    length, uses = numbers[0], numbers[1]
    count = q_ref.shape[0]

    def others(head, rows, columns):
        return [
            (parts[2 * at][rows, columns].astype(jnp.float32), to_rows(parts[2 * at + 1][head, :, rows]))
            for at in range(extra)
        ]

    def run(size, block):
        bonus = jnp.log2(jnp.full((ROWS, DH), uses, jnp.int32).astype(jnp.float32))
        for head in range(heads):
            columns = pl.ds(head * DH, DH)
            for start in range(0, count, ROWS):
                rows = pl.ds(start, ROWS)
                pieces = memory_pieces(mk_ref, mv_ref, columns, size, block, length)
                out, log = attend(q_ref[rows, columns], pieces)
                log = log + bonus
                if extra:
                    out, log = merge([(out, log)] + others(head, rows, columns))
                o_ref[rows, columns] = out.astype(o_ref.dtype)
                log_ref[head, :, rows] = to_row(log)

    @pl.when(uses > 0)
    def _():
        by_length(length, mk_ref.shape[0], run)

    @pl.when(uses == 0)
    def _():
        for head in range(heads):
            columns = pl.ds(head * DH, DH)
            for start in range(0, count, ROWS):
                rows = pl.ds(start, ROWS)
                if extra:
                    out, log = merge(others(head, rows, columns))
                    o_ref[rows, columns] = out.astype(o_ref.dtype)
                    log_ref[head, :, rows] = to_row(log)
                else:
                    o_ref[rows, columns] = jnp.zeros((ROWS, DH), o_ref.dtype)
                    log_ref[head, :, rows] = jnp.full((1, ROWS), NEVER, jnp.float32)


def final_kernel(heads, extra, *refs):
    o_ref = refs[-1]
    for head in range(heads):
        columns = pl.ds(head * DH, DH)
        for start in range(0, o_ref.shape[0], ROWS):
            rows = pl.ds(start, ROWS)
            parts = [
                (refs[2 * at][rows, columns].astype(jnp.float32), to_rows(refs[2 * at + 1][head, :, rows]))
                for at in range(extra)
            ]
            o_ref[rows, columns] = merge(parts)[0].astype(o_ref.dtype)


def per_device(
    queries, local_keys, local_values, mem_keys, mem_values, offsets, mem_lengths, out_weight
):
    count, width = queries.shape
    local_heads = width // DH
    memory_rows = mem_keys.shape[0]
    slots = offsets.shape[1]
    documents = lax.axis_size("doc")
    document = lax.axis_index("doc")
    core = document % 2
    side = (document // 2) % 2
    chunks = min(CHUNKS, local_heads)
    chunk_heads = local_heads // chunks
    heads = min(HEADS_PER_STEP, chunk_heads)
    steps = chunk_heads // heads
    block = heads * DH

    def permuted(values, target):
        pairs = [(source, target(source)) for source in range(documents)]
        return jax.tree.map(lambda value: lax.ppermute(value, "doc", pairs), values)

    down = lambda source: (source - slots) % documents
    up = lambda source: (source + slots) % documents
    across = lambda source: source ^ 2
    beside = lambda source: source ^ 1

    length = lax.dynamic_index_in_dim(mem_lengths, document, keepdims=False)
    table = lax.all_gather(offsets, "doc", axis=0, tiled=True)

    def numbers(distance):
        row = lax.dynamic_index_in_dim(table, (document + distance) % documents, keepdims=False)
        return jnp.stack([length, jnp.sum((row == distance).astype(jnp.int32))]).astype(jnp.int32)

    smem = pl.BlockSpec(memory_space=pltpu.SMEM)
    params = pltpu.CompilerParams(vmem_limit_bytes=VMEM)

    def flat(chunk, rows):
        return pl.BlockSpec((rows, block), lambda i: (0, chunk * steps + i))

    log_spec = pl.BlockSpec((heads, 1, count), lambda i: (i, 0, 0))
    part_shape = (
        jax.ShapeDtypeStruct((count, chunk_heads * DH), jnp.bfloat16),
        jax.ShapeDtypeStruct((chunk_heads, 1, count), jnp.float32),
    )
    part_specs = (flat(0, count), log_spec)

    def cost(keys):
        return pl.CostEstimate(
            flops=4 * count * keys * DH * chunk_heads * 2,
            bytes_accessed=4 * (count + keys) * DH * chunk_heads,
            transcendentals=count * keys * chunk_heads,
        )

    def near(chunk):
        return pl.pallas_call(
            functools.partial(near_kernel, heads),
            grid=(steps,),
            in_specs=[smem] + [flat(chunk, count)] * 3 + [flat(chunk, memory_rows)] * 2,
            out_specs=part_specs,
            out_shape=part_shape,
            compiler_params=params,
            cost_estimate=cost(count + memory_rows),
        )(length[None], queries, local_keys, local_values, mem_keys, mem_values)

    def visit(chunk, scalars, visiting, *parts):
        return pl.pallas_call(
            functools.partial(visit_kernel, heads, len(parts)),
            grid=(steps,),
            in_specs=[smem, flat(0, count)]
            + [flat(chunk, memory_rows)] * 2
            + list(part_specs) * len(parts),
            out_specs=part_specs,
            out_shape=part_shape,
            compiler_params=params,
            cost_estimate=cost(memory_rows),
        )(scalars, visiting, mem_keys, mem_values, *[x for part in parts for x in part])

    def final(*parts):
        return pl.pallas_call(
            functools.partial(final_kernel, heads, len(parts)),
            grid=(steps,),
            in_specs=list(part_specs) * len(parts),
            out_specs=part_specs[0],
            out_shape=part_shape[0],
            compiler_params=params,
            cost_estimate=pl.CostEstimate(
                flops=10 * count * chunk_heads * DH,
                bytes_accessed=2 * (len(parts) + 1) * count * chunk_heads * DH,
                transcendentals=4 * count * chunk_heads * DH,
            ),
        )(*[x for part in parts for x in part])

    def only(part, condition):
        return part[0], jnp.where(condition, part[1], NEVER)

    far = numbers(slots)
    middle = numbers(2)
    first = numbers(jnp.where(core == 0, 3, 1))
    second = numbers(jnp.where(core == 0, 1, 3))

    own = [queries[:, c * chunk_heads * DH : (c + 1) * chunk_heads * DH] for c in range(chunks)]
    ahead = [permuted(own[c], down) for c in range(chunks)]
    nears = [near(c) for c in range(chunks)]
    attended = []
    for c in range(chunks):
        swapped = permuted(jnp.where(side == 0, ahead[c], own[c]), across)
        visitor_one = permuted(swapped, beside)
        visitor_two = permuted(jnp.where(core == 0, ahead[c], own[c]), beside)
        back_one = permuted(visit(c, first, visitor_one), beside)
        back_two = permuted(visit(c, second, visitor_two), beside)
        back_across = permuted(visit(c, middle, swapped, back_one), across)
        back_far = permuted(
            visit(c, far, ahead[c], only(back_two, core == 0), only(back_across, side == 0)), up
        )
        attended.append(
            final(nears[c], back_far, only(back_two, core == 1), only(back_across, side == 1))
        )
    mixed = jnp.dot(
        jnp.concatenate(attended, axis=1), out_weight, preferred_element_type=jnp.float32
    )
    if lax.axis_size("head") != 2:
        return lax.psum_scatter(
            mixed.astype(jnp.bfloat16), "head", scatter_dimension=0, tiled=True
        )
    half = count // 2
    place = lax.axis_index("head")
    kept = lax.dynamic_slice_in_dim(mixed, place * half, half, 0)
    sent = lax.dynamic_slice_in_dim(mixed, (1 - place) * half, half, 0).astype(jnp.bfloat16)
    received = lax.ppermute(sent, "head", [(0, 1), (1, 0)])
    return (kept + received.astype(jnp.float32)).astype(jnp.bfloat16)


def solution(mesh):
    in_specs = (
        P("doc", "head"),
        P("doc", "head"),
        P("doc", "head"),
        P("doc", "head"),
        P("doc", "head"),
        P("doc", None),
        P(),
        P("head", None),
    )
    out_specs = P(("doc", "head"), None)
    return jax.shard_map(
        per_device, mesh=mesh, in_specs=in_specs, out_specs=out_specs, check_vma=False
    )
```

time: 567 us -> 294 us (0.52)
  matrix products: 213 us -> 9.4 us
  Pallas kernels: 0 us -> 115 us
  waiting for transfers between devices: 173 us -> 73.3 us
  other arithmetic: 84 us -> 11.2 us
  blocking collectives: 0 us -> 25.2 us
  local copies, waits for them, and re-layouts: 43 us -> 19.5 us
  between operations: 16.5 us -> 1.29 us
  starting transfers between devices: 27.3 us -> 33.4 us
    dot_general x11 -> x1, matrix products: 213 us -> 9.4 us  [per_device(): jnp.dot(jnp.concatenate(attended, axis=1), out_weight, preferred_element_...]
    pallas_call x0 -> x24, Pallas kernels: none -> 115 us  [the longest x16 76.2 us: visit(): pl.pallas_call(functools.partial(visit_kernel, heads, len(parts)), grid=(...]
    reduce_scatter x1 -> x0, waiting for transfers between devices: 91.2 us -> none  [per_device(): lax.psum_scatter(jnp.dot(attended, out_weight, preferred_element_type=jnp...]
    reduce_sum x4 -> x1, other arithmetic: 59.8 us -> 0.68 us  [numbers(): jnp.sum((row == distance).astype(jnp.int32))]
    all_gather x0 -> x1, blocking collectives: none -> 25.2 us  [per_device(): table = lax.all_gather(offsets, 'doc', axis=0, tiled=True)]
    reshape x5 -> x0, local copies, waits for them, and re-layouts: 20.9 us -> none  [split_heads(): return rows.reshape(rows.shape[0], local_heads, DH).transpose(1, 0, 2)]
    concatenate x3 -> x0, other arithmetic: 11.5 us -> none  [the longest x1 5.87 us: per_device(): jnp.concatenate([local_values, mem_values], axis=0)]
    ppermute x24 -> x49, waiting for transfers between devices: 82.1 us -> 73.3 us  [the longest x48 50.3 us: permuted(): return jax.tree.map(lambda value: lax.ppermute(value, 'doc', pairs), values)]
  transfers between devices with their start and end apart: 25 -> 49, of which waited for: 8 -> 8; matrix products, arithmetic and copies ran while one was open for 41% -> 3% of each run, Pallas kernels for 0% -> 39%
where the time goes in v1:
time: 294 us; the launch traced here: 288 us
  Pallas kernels  115 us (39%)
  waiting for transfers between devices  73.3 us (25%)
  starting transfers between devices  33.4 us (11%)
  blocking collectives  25.2 us (9%)
  local copies, waits for them, and re-layouts  19.5 us (7%)
  other arithmetic  11.2 us (4%)
  matrix products  9.4 us (3%)
    pallas_call x16, Pallas kernels, visit(): pl.pallas_call(functools.partial(visit_kernel, heads, len(parts)), grid=(...  76.2 us
    ppermute x48, waiting for transfers between devices, permuted(): return jax.tree.map(lambda value: lax.ppermute(value, 'doc', pairs), values)  50.3 us
    ppermute x48, starting transfers between devices, permuted(): return jax.tree.map(lambda value: lax.ppermute(value, 'doc', pairs), values)  31.8 us
    pallas_call x4, Pallas kernels, near(): pl.pallas_call(functools.partial(near_kernel, heads), grid=(steps,), in_s...  29.6 us
    all_gather x1, blocking collectives, per_device(): table = lax.all_gather(offsets, 'doc', axis=0, tiled=True)  25.2 us
    ppermute x1, waiting for transfers between devices, per_device(): received = lax.ppermute(sent, 'head', [(0, 1), (1, 0)])  22.9 us
    unnamed x78, local copies, waits for them, and re-layouts  15.5 us
    pallas_call x4, Pallas kernels, final(): pl.pallas_call(functools.partial(final_kernel, heads, len(parts)), grid=(...  9.44 us
  transfers between devices with their start and end apart: 49, of which 8 were waited for; matrix products, arithmetic and copies ran while one was open for 3% of the time, Pallas kernels for 39%

profile of v1, /device:TPU:0, one launch (start us, length us, event | category | flops | bytes accessed | tf_op | source)
XLA Modules:
  0.0 288.5 jit_solution(13104370306341384721)
XLA Ops:
  1.1 5.1 %collective-permute-start = (bf16[512,512]{1,0:T(8,128)(2,1)S(1)}, bf16[512,512]{1,0:T(8,128)(2,1)S(1)}, u32[]{:S(2)}, u32[]{:S(2)}) collective-permute-start(bf16[512,512]{1,0:T(8,128)(2,1)S(1)} %slice.12), channel_id=1, source_target_pairs={{0,24},{2,26},{4,28},{6,30},{8,0},{10,2},{12,4},{14,6},{16,8},{18,... | collective-permute-start | bytes 1572872 | tf_op jit(solution)/shard_map/ppermute | solution.py:180
  7.4 25.2 %all-gather = s32[16,1,4]{2,1,0:T(1,128)S(1)} all-gather(s32[1,1,4]{2,1,0:T(1,128)} %bitcast.6), channel_id=1, replica_groups=mesh['doc'=16,'head'=2] {'doc'}, dimensions={0}, use_global_device_ids=true | all-gather | bytes 272 | tf_op jit(solution)/shard_map/all_gather | solution.py:188
  37.8 7.2 %shard_map.82 = (bf16[512,512]{1,0:T(8,128)(2,1)S(1)}, f32[4,1,512]{2,1,0:T(1,128)S(1)}) custom-call(s32[1]{0:T(128)} %dynamic_slice.23.numbers, bf16[512,2048]{1,0:T(8,128)(2,1)S(1)} %copy-done.2, bf16[512,2048]{1,0:T(8,128)(2,1)S(1)} %copy-done.4, bf16[512,2048]{1,0:T(8,128)(2,1)} %lv_ref.7, bf16[1024,2048]{1,0:T(8,128)(2,1)} %mk_ref.39, ...), custom_call_target="tpu_custom_call" | custom-call | flops 3221225472 | bytes 4194304 | tf_op jit(solution)/shard_map/pallas_call | solution.py:215
  46.3 7.4 %shard_map.88 = (bf16[512,512]{1,0:T(8,128)(2,1)S(1)}, f32[4,1,512]{2,1,0:T(1,128)S(1)}) custom-call(s32[1]{0:T(128)} %dynamic_slice.23.numbers, bf16[512,2048]{1,0:T(8,128)(2,1)S(1)} %copy-done.2, bf16[512,2048]{1,0:T(8,128)(2,1)S(1)} %copy-done.4, bf16[512,2048]{1,0:T(8,128)(2,1)} %lv_ref.7, bf16[1024,2048]{1,0:T(8,128)(2,1)} %mk_ref.39, ...), custom_call_target="tpu_custom_call" | custom-call | flops 3221225472 | bytes 4194304 | tf_op jit(solution)/shard_map/pallas_call | solution.py:215
  60.1 11.2 %collective-permute-done.24.q_ref = bf16[512,512]{1,0:T(8,128)(2,1)S(1)} collective-permute-done((bf16[512,512]{1,0:T(8,128)(2,1)S(1)}, bf16[512,512]{1,0:T(8,128)(2,1)S(1)}, u32[]{:S(2)}, u32[]{:S(2)}) %collective-permute-start.24) | collective-permute-done | bytes 524320 | tf_op jit(solution)/shard_map/ppermute | solution.py:180
  71.3 10.6 %collective-permute-done.36.q_ref = bf16[512,512]{1,0:T(8,128)(2,1)S(1)} collective-permute-done((bf16[512,512]{1,0:T(8,128)(2,1)S(1)}, bf16[512,512]{1,0:T(8,128)(2,1)S(1)}, u32[]{:S(2)}, u32[]{:S(2)}) %collective-permute-start.36) | collective-permute-done | bytes 524320 | tf_op jit(solution)/shard_map/ppermute | solution.py:180
  84.5 5.0 %shard_map.83 = (bf16[512,512]{1,0:T(8,128)(2,1)S(1)}, f32[4,1,512]{2,1,0:T(1,128)S(1)}) custom-call(s32[2]{0:T(128)S(1)} %pad_add_fusion.1.numbers, bf16[512,512]{1,0:T(8,128)(2,1)S(1)} %collective-permute-done.1.q_ref, bf16[1024,2048]{1,0:T(8,128)(2,1)S(1)} %copy-done, bf16[1024,2048]{1,0:T(8,128)(2,1)} %mv_ref.39), custom_call_target="tpu_custom_call" | custom-call | flops 2147483648 | bytes 3145728 | tf_op jit(solution)/shard_map/pallas_call | solution.py:226
  97.0 4.8 %shard_map.89 = (bf16[512,512]{1,0:T(8,128)(2,1)S(1)}, f32[4,1,512]{2,1,0:T(1,128)S(1)}) custom-call(s32[2]{0:T(128)S(1)} %pad_add_fusion.1.numbers, bf16[512,512]{1,0:T(8,128)(2,1)S(1)} %collective-permute-done.13.q_ref, bf16[1024,2048]{1,0:T(8,128)(2,1)S(1)} %copy-done.1, bf16[1024,2048]{1,0:T(8,128)(2,1)} %mv_ref.39), custom_call_target="tpu_custom_call" | custom-call | flops 2147483648 | bytes 3145728 | tf_op jit(solution)/shard_map/pallas_call | solution.py:226
  101.9 5.3 %shard_map.84 = (bf16[512,512]{1,0:T(8,128)(2,1)S(1)}, f32[4,1,512]{2,1,0:T(1,128)S(1)}) custom-call(s32[2]{0:T(128)S(1)} %pad_add_fusion.3.numbers, bf16[512,512]{1,0:T(8,128)(2,1)} %collective-permute-done.5.q_ref, bf16[1024,2048]{1,0:T(8,128)(2,1)S(1)} %copy-done.1, bf16[1024,2048]{1,0:T(8,128)(2,1)} %mv_ref.39), custom_call_target="tpu_custom_call" | custom-call | flops 2147483648 | bytes 3145728 | tf_op jit(solution)/shard_map/pallas_call | solution.py:226
  112.6 4.9 %shard_map.101 = (bf16[512,512]{1,0:T(8,128)(2,1)S(1)}, f32[4,1,512]{2,1,0:T(1,128)S(1)}) custom-call(s32[2]{0:T(128)S(1)} %pad_add_fusion.1.numbers, bf16[512,512]{1,0:T(8,128)(2,1)S(1)} %collective-permute-done.37.q_ref, bf16[1024,2048]{1,0:T(8,128)(2,1)S(1)} %copy-done.1, bf16[1024,2048]{1,0:T(8,128)(2,1)} %mv_ref.39), custom_call_target="tpu_custom_call" | custom-call | flops 2147483648 | bytes 3145728 | tf_op jit(solution)/shard_map/pallas_call | solution.py:226
  119.6 9.5 %collective-permute-done.40.q_ref = bf16[512,512]{1,0:T(8,128)(2,1)S(1)} collective-permute-done((bf16[512,512]{1,0:T(8,128)(2,1)S(1)}, bf16[512,512]{1,0:T(8,128)(2,1)S(1)}, u32[]{:S(2)}, u32[]{:S(2)}) %collective-permute-start.40) | collective-permute-done | bytes 524320 | tf_op jit(solution)/shard_map/ppermute | solution.py:180
  129.7 5.1 %shard_map.85 = (bf16[512,512]{1,0:T(8,128)(2,1)S(1)}, f32[4,1,512]{2,1,0:T(1,128)S(1)}) custom-call(s32[2]{0:T(128)S(1)} %pad_add_fusion.2.numbers, bf16[512,512]{1,0:T(8,128)(2,1)S(1)} %collective-permute-done.4.q_ref, bf16[1024,2048]{1,0:T(8,128)(2,1)S(1)} %copy-done.1, bf16[1024,2048]{1,0:T(8,128)(2,1)} %mv_ref.39, ...), custom_call_target="tpu_custom_call" | custom-call | flops 2147483648 | bytes 3145728 | tf_op jit(solution)/shard_map/pallas_call | solution.py:226
  134.9 5.7 %shard_map.90 = (bf16[512,512]{1,0:T(8,128)(2,1)}, f32[4,1,512]{2,1,0:T(1,128)S(1)}) custom-call(s32[2]{0:T(128)S(1)} %pad_add_fusion.3.numbers, bf16[512,512]{1,0:T(8,128)(2,1)S(1)} %collective-permute-done.17.q_ref, bf16[1024,2048]{1,0:T(8,128)(2,1)S(1)} %copy-done.1, bf16[1024,2048]{1,0:T(8,128)(2,1)} %mv_ref.39), custom_call_target="tpu_custom_call" | custom-call | flops 2147483648 | bytes 3145728 | tf_op jit(solution)/shard_map/pallas_call | solution.py:226
  146.0 5.2 %shard_map.102 = (bf16[512,512]{1,0:T(8,128)(2,1)S(1)}, f32[4,1,512]{2,1,0:T(1,128)S(1)}) custom-call(s32[2]{0:T(128)S(1)} %pad_add_fusion.3.numbers, bf16[512,512]{1,0:T(8,128)(2,1)S(1)} %collective-permute-done.41.q_ref, bf16[1024,2048]{1,0:T(8,128)(2,1)S(1)} %copy-done.1, bf16[1024,2048]{1,0:T(8,128)(2,1)} %mv_ref.39), custom_call_target="tpu_custom_call" | custom-call | flops 2147483648 | bytes 3145728 | tf_op jit(solution)/shard_map/pallas_call | solution.py:226
  152.0 5.2 %shard_map.91 = (bf16[512,512]{1,0:T(8,128)(2,1)S(1)}, f32[4,1,512]{2,1,0:T(1,128)S(1)}) custom-call(s32[2]{0:T(128)S(1)} %pad_add_fusion.2.numbers, bf16[512,512]{1,0:T(8,128)(2,1)S(1)} %collective-permute-done.16.q_ref, bf16[1024,2048]{1,0:T(8,128)(2,1)S(1)} %copy-done.1, bf16[1024,2048]{1,0:T(8,128)(2,1)} %mv_ref.39, ...), custom_call_target="tpu_custom_call" | custom-call | flops 2147483648 | bytes 3145728 | tf_op jit(solution)/shard_map/pallas_call | solution.py:226
  157.7 5.3 %shard_map.97 = (bf16[512,512]{1,0:T(8,128)(2,1)S(1)}, f32[4,1,512]{2,1,0:T(1,128)S(1)}) custom-call(s32[2]{0:T(128)S(1)} %pad_add_fusion.2.numbers, bf16[512,512]{1,0:T(8,128)(2,1)S(1)} %collective-permute-done.28.q_ref, bf16[1024,2048]{1,0:T(8,128)(2,1)S(1)} %copy-done.1, bf16[1024,2048]{1,0:T(8,128)(2,1)} %mv_ref.39, ...), custom_call_target="tpu_custom_call" | custom-call | flops 2147483648 | bytes 3145728 | tf_op jit(solution)/shard_map/pallas_call | solution.py:226
  163.3 5.2 %shard_map.103 = (bf16[512,512]{1,0:T(8,128)(2,1)S(1)}, f32[4,1,512]{2,1,0:T(1,128)S(1)}) custom-call(s32[2]{0:T(128)S(1)} %pad_add_fusion.2.numbers, bf16[512,512]{1,0:T(8,128)(2,1)S(1)} %collective-permute-done.40.q_ref, bf16[1024,2048]{1,0:T(8,128)(2,1)S(1)} %copy-done.1, bf16[1024,2048]{1,0:T(8,128)(2,1)} %mv_ref.39, ...), custom_call_target="tpu_custom_call" | custom-call | flops 2147483648 | bytes 3145728 | tf_op jit(solution)/shard_map/pallas_call | solution.py:226
  175.4 8.2 %collective-permute-done.33 = f32[4,1,512]{2,1,0:T(1,128)S(1)} collective-permute-done((f32[4,1,512]{2,1,0:T(1,128)S(1)}, f32[4,1,512]{2,1,0:T(1,128)S(1)}, u32[]{:S(2)}, u32[]{:S(2)}) %collective-permute-start.33) | collective-permute-done | bytes 8224 | tf_op jit(solution)/shard_map/ppermute | solution.py:180
  184.2 7.3 %collective-permute-done.45 = f32[4,1,512]{2,1,0:T(1,128)S(1)} collective-permute-done((f32[4,1,512]{2,1,0:T(1,128)S(1)}, f32[4,1,512]{2,1,0:T(1,128)S(1)}, u32[]{:S(2)}, u32[]{:S(2)}) %collective-permute-start.45) | collective-permute-done | bytes 8224 | tf_op jit(solution)/shard_map/ppermute | solution.py:180
  197.2 5.4 %collective-permute-start.22 = (bf16[512,512]{1,0:T(8,128)(2,1)}, bf16[512,512]{1,0:T(8,128)(2,1)}, u32[]{:S(2)}, u32[]{:S(2)}) collective-permute-start(bf16[512,512]{1,0:T(8,128)(2,1)} %get-tuple-element.63), channel_id=1, source_target_pairs={{0,8},{2,10},{4,12},{6,14},{8,16},{10,18},{12,20},{14,22},{16,24},... | collective-permute-start | bytes 1572872 | tf_op jit(solution)/shard_map/ppermute | solution.py:180
  213.9 7.5 %shard_map.94 = (bf16[512,512]{1,0:T(8,128)(2,1)S(1)}, f32[4,1,512]{2,1,0:T(1,128)S(1)}) custom-call(s32[1]{0:T(128)} %dynamic_slice.23.numbers, bf16[512,2048]{1,0:T(8,128)(2,1)S(1)} %copy-done.3, bf16[512,2048]{1,0:T(8,128)(2,1)S(1)} %copy-done.5, bf16[512,2048]{1,0:T(8,128)(2,1)} %lv_ref.7, bf16[1024,2048]{1,0:T(8,128)(2,1)} %mk_ref.39, ...), custom_call_target="tpu_custom_call" | custom-call | flops 3221225472 | bytes 4194304 | tf_op jit(solution)/shard_map/pallas_call | solution.py:215
  226.3 7.5 %shard_map.100 = (bf16[512,512]{1,0:T(8,128)(2,1)S(1)}, f32[4,1,512]{2,1,0:T(1,128)S(1)}) custom-call(s32[1]{0:T(128)} %dynamic_slice.23.numbers, bf16[512,2048]{1,0:T(8,128)(2,1)S(1)} %copy-done.3, bf16[512,2048]{1,0:T(8,128)(2,1)S(1)} %copy-done.5, bf16[512,2048]{1,0:T(8,128)(2,1)} %lv_ref.7, bf16[1024,2048]{1,0:T(8,128)(2,1)} %mk_ref.39, ...), custom_call_target="tpu_custom_call" | custom-call | flops 3221225472 | bytes 4194304 | tf_op jit(solution)/shard_map/pallas_call | solution.py:215
  249.5 9.4 %fusion = f32[512,2048]{1,0:T(8,128)} fusion(bf16[2048,2048]{1,0:T(8,128)(2,1)} %param.15, bf16[512,512]{1,0:T(8,128)(2,1)S(1)} %shard_map.105, bf16[512,512]{1,0:T(8,128)(2,1)S(1)} %shard_map.99, bf16[512,512]{1,0:T(8,128)(2,1)S(1)} %shard_map.93, bf16[512,512]{1,0:T(8,128)(2,1)S(1)} %shard_map.87), kind=kOutput, calls=%fused_computation | convolution fusion | flops 4303355904 | bytes 14680064 | tf_op jit(solution)/shard_map/dot_general | solution.py:278
  262.2 22.9 %collective-permute-done.48 = bf16[256,2048]{1,0:T(8,128)(2,1)S(1)} collective-permute-done((bf16[256,2048]{1,0:T(8,128)(2,1)S(1)}, bf16[256,2048]{1,0:T(8,128)(2,1)S(1)}, u32[]{:S(2)}, u32[]{:S(2)}) %collective-permute-start.48) | collective-permute-done | bytes 1048608 | tf_op jit(solution)/shard_map/ppermute | solution.py:289
  (197 shorter events, 91.0 us)
Async XLA Ops:
  1.1 44.0 %collective-permute-start = (bf16[512,512]{1,0:T(8,128)(2,1)S(1)}, bf16[512,512]{1,0:T(8,128)(2,1)S(1)}, u32[]{:S(2)}, u32[]{:S(2)}) collective-permute-start(bf16[512,512]{1,0:T(8,128)(2,1)S(1)} %slice.12), channel_id=1, source_target_pairs={{0,24},{2,26},{4,28},{6,30},{8,0},{10,2},{12,4},{14,6},{16,8},{18,... | collective-permute-start | bytes 1572872 | tf_op jit(solution)/shard_map/ppermute | solution.py:180
  45.4 26.0 %collective-permute-start.24 = (bf16[512,512]{1,0:T(8,128)(2,1)S(1)}, bf16[512,512]{1,0:T(8,128)(2,1)S(1)}, u32[]{:S(2)}, u32[]{:S(2)}) collective-permute-start(bf16[512,512]{1,0:T(8,128)(2,1)S(1)} %get-tuple-element.97), channel_id=1, source_target_pairs={{0,24},{2,26},{4,28},{6,30},{8,0},{10,2},{12,4},{14,6},{16,8},{18,... | collective-permute-start | bytes 1572872 | tf_op jit(solution)/shard_map/ppermute | solution.py:180
  46.1 35.9 %collective-permute-start.36 = (bf16[512,512]{1,0:T(8,128)(2,1)S(1)}, bf16[512,512]{1,0:T(8,128)(2,1)S(1)}, u32[]{:S(2)}, u32[]{:S(2)}) collective-permute-start(bf16[512,512]{1,0:T(8,128)(2,1)S(1)} %get-tuple-element.99), channel_id=1, source_target_pairs={{0,24},{2,26},{4,28},{6,30},{8,0},{10,2},{12,4},{14,6},{16,8},{18,... | collective-permute-start | bytes 1572872 | tf_op jit(solution)/shard_map/ppermute | solution.py:180
  53.7 30.8 %collective-permute-start.1 = (bf16[512,512]{1,0:T(8,128)(2,1)S(1)}, bf16[512,512]{1,0:T(8,128)(2,1)S(1)}, u32[]{:S(2)}, u32[]{:S(2)}) collective-permute-start(bf16[512,512]{1,0:T(8,128)(2,1)S(1)} %get-tuple-element.90), channel_id=1, source_target_pairs={{0,2},{2,0},{4,6},{6,4},{8,10},{10,8},{12,14},{14,12},{16,18},{18,... | collective-permute-start | bytes 1572872 | tf_op jit(solution)/shard_map/ppermute | solution.py:180
  57.2 33.6 %collective-permute-start.4 = (bf16[512,512]{1,0:T(8,128)(2,1)S(1)}, bf16[512,512]{1,0:T(8,128)(2,1)S(1)}, u32[]{:S(2)}, u32[]{:S(2)}) collective-permute-start(bf16[512,512]{1,0:T(8,128)(2,1)S(1)} %get-tuple-element.89), channel_id=1, source_target_pairs={{0,4},{2,6},{4,0},{6,2},{8,12},{10,14},{12,8},{14,10},{16,20},{18,... | collective-permute-start | bytes 1572872 | tf_op jit(solution)/shard_map/ppermute | solution.py:180
  92.1 25.6 %collective-permute-start.16 = (bf16[512,512]{1,0:T(8,128)(2,1)}, bf16[512,512]{1,0:T(8,128)(2,1)S(1)}, u32[]{:S(2)}, u32[]{:S(2)}) collective-permute-start(bf16[512,512]{1,0:T(8,128)(2,1)} %get-tuple-element.91), channel_id=1, source_target_pairs={{0,4},{2,6},{4,0},{6,2},{8,12},{10,14},{12,8},{14,10},{16,20},{18,... | collective-permute-start | bytes 1572872 | tf_op jit(solution)/shard_map/ppermute | solution.py:180
  92.2 26.9 %collective-permute-start.28 = (bf16[512,512]{1,0:T(8,128)(2,1)}, bf16[512,512]{1,0:T(8,128)(2,1)S(1)}, u32[]{:S(2)}, u32[]{:S(2)}) collective-permute-start(bf16[512,512]{1,0:T(8,128)(2,1)} %get-tuple-element.101), channel_id=1, source_target_pairs={{0,4},{2,6},{4,0},{6,2},{8,12},{10,14},{12,8},{14,10},{16,20},{18,... | collective-permute-start | bytes 1572872 | tf_op jit(solution)/shard_map/ppermute | solution.py:180
  94.2 17.9 %collective-permute-start.37 = (bf16[512,512]{1,0:T(8,128)(2,1)}, bf16[512,512]{1,0:T(8,128)(2,1)S(1)}, u32[]{:S(2)}, u32[]{:S(2)}) collective-permute-start(bf16[512,512]{1,0:T(8,128)(2,1)} %get-tuple-element.102), channel_id=1, source_target_pairs={{0,2},{2,0},{4,6},{6,4},{8,10},{10,8},{12,14},{14,12},{16,18},{18,... | collective-permute-start | bytes 1572872 | tf_op jit(solution)/shard_map/ppermute | solution.py:180
  101.8 27.3 %collective-permute-start.40 = (bf16[512,512]{1,0:T(8,128)(2,1)S(1)}, bf16[512,512]{1,0:T(8,128)(2,1)S(1)}, u32[]{:S(2)}, u32[]{:S(2)}) collective-permute-start(bf16[512,512]{1,0:T(8,128)(2,1)S(1)} %copy-done.38), channel_id=1, source_target_pairs={{0,4},{2,6},{4,0},{6,2},{8,12},{10,14},{12,8},{14,10},{16,20},{18,... | collective-permute-start | bytes 1572872 | tf_op jit(solution)/shard_map/ppermute | solution.py:180
  107.2 22.5 %collective-permute-start.6 = (bf16[512,512]{1,0:T(8,128)(2,1)S(1)}, bf16[512,512]{1,0:T(8,128)(2,1)S(1)}, u32[]{:S(2)}, u32[]{:S(2)}) collective-permute-start(bf16[512,512]{1,0:T(8,128)(2,1)S(1)} %get-tuple-element.49), channel_id=1, source_target_pairs={{0,2},{2,0},{4,6},{6,4},{8,10},{10,8},{12,14},{14,12},{16,18},{18,... | collective-permute-start | bytes 1572872 | tf_op jit(solution)/shard_map/ppermute | solution.py:180
  119.4 21.2 %collective-permute-start.29 = (bf16[512,512]{1,0:T(8,128)(2,1)S(1)}, bf16[512,512]{1,0:T(8,128)(2,1)S(1)}, u32[]{:S(2)}, u32[]{:S(2)}) collective-permute-start(bf16[512,512]{1,0:T(8,128)(2,1)S(1)} %collective-permute-done.28.q_ref), channel_id=1, source_target_pairs={{0,2},{2,0},{4,6},{6,4},{8,10},{10,8},{12,14},{14,12},{16,18},{18,... | collective-permute-start | bytes 1572872 | tf_op jit(solution)/shard_map/ppermute | solution.py:180
  129.2 39.3 %collective-permute-start.2 = (bf16[512,512]{1,0:T(8,128)(2,1)S(1)}, bf16[512,512]{1,0:T(8,128)(2,1)S(1)}, u32[]{:S(2)}, u32[]{:S(2)}) collective-permute-start(bf16[512,512]{1,0:T(8,128)(2,1)S(1)} %copy-done.37), channel_id=1, source_target_pairs={{0,2},{2,0},{4,6},{6,4},{8,10},{10,8},{12,14},{14,12},{16,18},{18,... | collective-permute-start | bytes 1572872 | tf_op jit(solution)/shard_map/ppermute | solution.py:180
  157.2 26.9 %collective-permute-start.14 = (bf16[512,512]{1,0:T(8,128)(2,1)S(1)}, bf16[512,512]{1,0:T(8,128)(2,1)S(1)}, u32[]{:S(2)}, u32[]{:S(2)}) collective-permute-start(bf16[512,512]{1,0:T(8,128)(2,1)S(1)} %get-tuple-element.57), channel_id=1, source_target_pairs={{0,2},{2,0},{4,6},{6,4},{8,10},{10,8},{12,14},{14,12},{16,18},{18,... | collective-permute-start | bytes 1572872 | tf_op jit(solution)/shard_map/ppermute | solution.py:180
  163.1 34.0 %collective-permute-start.26 = (bf16[512,512]{1,0:T(8,128)(2,1)S(1)}, bf16[512,512]{1,0:T(8,128)(2,1)S(1)}, u32[]{:S(2)}, u32[]{:S(2)}) collective-permute-start(bf16[512,512]{1,0:T(8,128)(2,1)S(1)} %get-tuple-element.67), channel_id=1, source_target_pairs={{0,2},{2,0},{4,6},{6,4},{8,10},{10,8},{12,14},{14,12},{16,18},{18,... | collective-permute-start | bytes 1572872 | tf_op jit(solution)/shard_map/ppermute | solution.py:180
  168.5 24.7 %collective-permute-start.20 = (bf16[512,512]{1,0:T(8,128)(2,1)S(1)}, bf16[512,512]{1,0:T(8,128)(2,1)S(1)}, u32[]{:S(2)}, u32[]{:S(2)}) collective-permute-start(bf16[512,512]{1,0:T(8,128)(2,1)S(1)} %get-tuple-element.61), channel_id=1, source_target_pairs={{0,4},{2,6},{4,0},{6,2},{8,12},{10,14},{12,8},{14,10},{16,20},{18,... | collective-permute-start | bytes 1572872 | tf_op jit(solution)/shard_map/ppermute | solution.py:180
  173.7 23.5 %collective-permute-start.32 = (bf16[512,512]{1,0:T(8,128)(2,1)S(1)}, bf16[512,512]{1,0:T(8,128)(2,1)S(1)}, u32[]{:S(2)}, u32[]{:S(2)}) collective-permute-start(bf16[512,512]{1,0:T(8,128)(2,1)S(1)} %get-tuple-element.71), channel_id=1, source_target_pairs={{0,4},{2,6},{4,0},{6,2},{8,12},{10,14},{12,8},{14,10},{16,20},{18,... | collective-permute-start | bytes 1572872 | tf_op jit(solution)/shard_map/ppermute | solution.py:180
  184.1 22.7 %collective-permute-start.38 = (bf16[512,512]{1,0:T(8,128)(2,1)S(1)}, bf16[512,512]{1,0:T(8,128)(2,1)S(1)}, u32[]{:S(2)}, u32[]{:S(2)}) collective-permute-start(bf16[512,512]{1,0:T(8,128)(2,1)S(1)} %get-tuple-element.77), channel_id=1, source_target_pairs={{0,2},{2,0},{4,6},{6,4},{8,10},{10,8},{12,14},{14,12},{16,18},{18,... | collective-permute-start | bytes 1572872 | tf_op jit(solution)/shard_map/ppermute | solution.py:180
  193.2 29.0 %collective-permute-start.10 = (bf16[512,512]{1,0:T(8,128)(2,1)S(1)}, bf16[512,512]{1,0:T(8,128)(2,1)S(1)}, u32[]{:S(2)}, u32[]{:S(2)}) collective-permute-start(bf16[512,512]{1,0:T(8,128)(2,1)S(1)} %get-tuple-element.53), channel_id=1, source_target_pairs={{0,8},{2,10},{4,12},{6,14},{8,16},{10,18},{12,20},{14,22},{16,24},... | collective-permute-start | bytes 1572872 | tf_op jit(solution)/shard_map/ppermute | solution.py:180
  197.2 41.3 %collective-permute-start.22 = (bf16[512,512]{1,0:T(8,128)(2,1)}, bf16[512,512]{1,0:T(8,128)(2,1)}, u32[]{:S(2)}, u32[]{:S(2)}) collective-permute-start(bf16[512,512]{1,0:T(8,128)(2,1)} %get-tuple-element.63), channel_id=1, source_target_pairs={{0,8},{2,10},{4,12},{6,14},{8,16},{10,18},{12,20},{14,22},{16,24},... | collective-permute-start | bytes 1572872 | tf_op jit(solution)/shard_map/ppermute | solution.py:180
  208.5 35.8 %collective-permute-start.34 = (bf16[512,512]{1,0:T(8,128)(2,1)}, bf16[512,512]{1,0:T(8,128)(2,1)}, u32[]{:S(2)}, u32[]{:S(2)}) collective-permute-start(bf16[512,512]{1,0:T(8,128)(2,1)} %get-tuple-element.73), channel_id=1, source_target_pairs={{0,8},{2,10},{4,12},{6,14},{8,16},{10,18},{12,20},{14,22},{16,24},... | collective-permute-start | bytes 1572872 | tf_op jit(solution)/shard_map/ppermute | solution.py:180
  212.6 34.4 %collective-permute-start.46 = (bf16[512,512]{1,0:T(8,128)(2,1)}, bf16[512,512]{1,0:T(8,128)(2,1)}, u32[]{:S(2)}, u32[]{:S(2)}) collective-permute-start(bf16[512,512]{1,0:T(8,128)(2,1)} %get-tuple-element.83), channel_id=1, source_target_pairs={{0,8},{2,10},{4,12},{6,14},{8,16},{10,18},{12,20},{14,22},{16,24},... | collective-permute-start | bytes 1572872 | tf_op jit(solution)/shard_map/ppermute | solution.py:180
  223.0 21.3 %collective-permute-start.35 = (f32[4,1,512]{2,1,0:T(1,128)S(1)}, f32[4,1,512]{2,1,0:T(1,128)S(1)}, u32[]{:S(2)}, u32[]{:S(2)}) collective-permute-start(f32[4,1,512]{2,1,0:T(1,128)S(1)} %get-tuple-element.74), channel_id=1, source_target_pairs={{0,8},{2,10},{4,12},{6,14},{8,16},{10,18},{12,20},{14,22},{16,24},... | collective-permute-start | bytes 24584 | tf_op jit(solution)/shard_map/ppermute | solution.py:180
  223.8 23.1 %collective-permute-start.47 = (f32[4,1,512]{2,1,0:T(1,128)S(1)}, f32[4,1,512]{2,1,0:T(1,128)S(1)}, u32[]{:S(2)}, u32[]{:S(2)}) collective-permute-start(f32[4,1,512]{2,1,0:T(1,128)S(1)} %get-tuple-element.84), channel_id=1, source_target_pairs={{0,8},{2,10},{4,12},{6,14},{8,16},{10,18},{12,20},{14,22},{16,24},... | collective-permute-start | bytes 24584 | tf_op jit(solution)/shard_map/ppermute | solution.py:180
  260.7 24.5 %collective-permute-start.48 = (bf16[256,2048]{1,0:T(8,128)(2,1)S(1)}, bf16[256,2048]{1,0:T(8,128)(2,1)S(1)}, u32[]{:S(2)}, u32[]{:S(2)}) collective-permute-start(bf16[256,2048]{1,0:T(8,128)(2,1)S(1)} %dynamic-slice_convert_fusion), channel_id=1, source_target_pairs={{0,1},{1,0},{2,3},{3,2},{4,5},{5,4},{6,7},{7,6},{8,9},{9,8},{10,11... | collective-permute-start | bytes 3145736 | tf_op jit(solution)/shard_map/ppermute | solution.py:289
  (64 other events, 619.1 us)
